TPU v7x, 32 devices: a whole 2x2x4 slice. The times are simulated.
32 devices in a mesh: lon: 4 (over y, x), lat: 8 (over z, core).
Axes of the slice: x: 2, y: 2, z: 4, core: 2. Of those that a mesh axis runs over, the one named last changes fastest.
Arguments:
- tracers: float32 [4, 16, 1024, 512], P(None, None, 'lat', 'lon'), may hold values from -6 to 6
- fill_fraction: float32 [16, 1024, 512], P(None, 'lat', 'lon'), may hold values from 0.3 to 1
- ocean_mask: int32 [16, 1024, 512], P(None, 'lat', 'lon'), may hold values 0 or 1
- east_speed: float32 [16, 1024, 512], P(None, 'lat', 'lon'), may hold values from -3 to 3
- north_speed: float32 [16, 1024, 512], P(None, 'lat', 'lon'), may hold values from -3 to 3
- diffusivity: float32 [16], replicated, may hold values from 0.1 to 1
- cell_area: float32 [1024, 512], P('lat', 'lon'), may hold values from 0.25 to 1
- owner_map: int32 [4096, 1], P(('lon', 'lat')), may hold values from 0 to 31; in each aligned block of 128 rows (0 to 127, 128 to 255, ...) at most 8 rows name the same one
Outputs:
- updated: float32 [4, 16, 1024, 512], P(None, None, 'lat', 'lon')
- received_two: float32 [32, 256, 2048], P(('lon', 'lat'))
- received_four: float32 [32, 256, 512], P(('lon', 'lat'))
Inputs may be any that keep to these rules, and one draw needn't show every extreme that they name: `owner_map`: owner device numbers in lon-major order. Of the 128 rows of one device, at most 8 name the same owner, and in some device exactly 8 do.
All inputs are finite; a program needn't handle non-finite values. No bound on the sum of `ocean_mask` on one device may be relied on, other than what follows from the above.
Results may differ from a plain program's by a relative error of at most 0.00007.
Values sent between devices are 32-bit elements; how exact they have to be, the bound alone decides.
A program may use at most 128 MiB of HBM per device.

v0:
```python
import jax
import jax.numpy as jnp
from jax import lax
from jax.sharding import PartitionSpec as P

BAND_ROWS = 16


time_step = 0.05
depth_floor = 0.25
weight_floor = 0.25


def padded(block, sides, width, periodic):
    for axis, dim in sides:
        count = lax.axis_size(axis)
        forward = [(i, i + 1) for i in range(count - 1)]
        if periodic:
            forward.append((count - 1, 0))
        backward = [(target, source) for source, target in forward]
        low = lax.ppermute(
            lax.slice_in_dim(block, block.shape[dim] - width, None, axis=dim), axis, forward
        )
        high = lax.ppermute(lax.slice_in_dim(block, 0, width, axis=dim), axis, backward)
        block = jnp.concatenate([low, block, high], axis=dim)
    return block


def partner_2(block, axis, stride):
    count = lax.axis_size(axis)
    route = []
    for low in range(count):
        high = low | 1 << stride
        if high != low and high < count:
            route += [(low, high), (high, low)]
    return lax.ppermute(block, axis, route)


def face_flux(lower_val, upper_val, lower_h, upper_h, lower_speed, upper_speed, mixing):
    open_depth = jnp.minimum(lower_h, upper_h)
    face_speed = 0.5 * (lower_speed + upper_speed)
    return open_depth * (
        0.5 * face_speed * (lower_val + upper_val)
        - 0.5 * jnp.abs(face_speed) * (upper_val - lower_val)
        - mixing * (upper_val - lower_val)
    )


def pool_pairs(field):
    old_shape = field.shape
    return field.reshape(old_shape[:-2] + (old_shape[-2] // 2, 2, old_shape[-1] // 2, 2)).sum(
        axis=(-3, -1)
    )


def coarsen(updated, weight):
    weighted = pool_pairs(updated * weight[None])
    weight_two = pool_pairs(weight)
    weighted_four = pool_pairs(weighted)
    weight_four = pool_pairs(weight_two)
    coarse_two = weighted / jnp.maximum(weight_two, weight_floor)[None]
    coarse_four = weighted_four / jnp.maximum(weight_four, weight_floor)[None]
    return (coarse_two, coarse_four)


def band_blocks(field, band):
    shape_of = field.shape
    bands = shape_of[2] // band
    split = field.reshape(shape_of[0], shape_of[1], bands, band, shape_of[3])
    return split.transpose(1, 2, 0, 3, 4).reshape(
        shape_of[1] * bands, shape_of[0] * band * shape_of[3]
    )


def column_edges(field):
    return jnp.concatenate([field[..., :1], field[..., -1:]], axis=-1)


def row_edges(field):
    return jnp.concatenate([field[..., :1, :], field[..., -1:, :]], axis=-2)


def shifted_east(field, column):
    return jnp.concatenate([field[..., 1:], column[..., None]], axis=-1)


def shifted_north(field, row):
    return jnp.concatenate([field[..., 1:, :], row[..., None, :]], axis=-2)


def local(
    tracers, fill_fraction, ocean_mask, east_speed, north_speed, diffusivity, cell_area, owner_map
):
    wet_depth = fill_fraction * ocean_mask.astype(jnp.float32)
    mixing = diffusivity[:, None, None]
    mixing_edge = diffusivity[:, None]
    count_tr = tracers.shape[0]
    lon_pack = jnp.concatenate(
        [column_edges(tracers), column_edges(wet_depth)[None], column_edges(east_speed)[None]],
        axis=0,
    )
    lon_got = padded(lon_pack, (("lon", 3),), 1, True)
    west_col = lon_got[..., 0]
    east_col = lon_got[..., 3]
    lat_pack = jnp.concatenate(
        [row_edges(tracers), row_edges(wet_depth)[None], row_edges(north_speed)[None]], axis=0
    )
    lat_got = padded(lat_pack, (("lat", 2),), 1, False)
    south_row = lat_got[:, :, 0, :]
    north_row = lat_got[:, :, 3, :]
    partner = lat_pack[:, :, 1, :]
    for bit_index in range(lax.axis_size("lon").bit_length() - 1):
        partner = partner_2(partner, "lon", bit_index)
    folded = jnp.flip(partner, axis=-1)
    fold_sign = jnp.concatenate(
        [jnp.ones((count_tr + 1,), jnp.float32), -jnp.ones((1,), jnp.float32)]
    )
    folded = folded * fold_sign[:, None, None]
    at_fold = lax.axis_index("lat") == lax.axis_size("lat") - 1
    north_row = jnp.where(at_fold, folded, north_row)
    east_flux = face_flux(
        tracers,
        shifted_east(tracers, east_col[:count_tr]),
        wet_depth,
        shifted_east(wet_depth, east_col[count_tr]),
        east_speed,
        shifted_east(east_speed, east_col[count_tr + 1]),
        mixing,
    )
    west_face = face_flux(
        west_col[:count_tr],
        tracers[..., 0],
        west_col[count_tr],
        wet_depth[..., 0],
        west_col[count_tr + 1],
        east_speed[..., 0],
        mixing_edge,
    )
    west_flux = jnp.concatenate([west_face[..., None], east_flux[..., :-1]], axis=-1)
    north_flux = face_flux(
        tracers,
        shifted_north(tracers, north_row[:count_tr]),
        wet_depth,
        shifted_north(wet_depth, north_row[count_tr]),
        north_speed,
        shifted_north(north_speed, north_row[count_tr + 1]),
        mixing,
    )
    south_face = face_flux(
        south_row[:count_tr],
        tracers[:, :, 0, :],
        south_row[count_tr],
        wet_depth[:, 0, :],
        south_row[count_tr + 1],
        north_speed[:, 0, :],
        mixing_edge,
    )
    south_flux = jnp.concatenate([south_face[:, :, None, :], north_flux[:, :, :-1, :]], axis=-2)
    volume = cell_area[None] * jnp.maximum(wet_depth, depth_floor)
    updated = tracers + time_step * (west_flux - east_flux + (south_flux - north_flux)) / volume
    coarse_two, coarse_four = coarsen(updated, cell_area[None] * wet_depth)
    blocks_two = band_blocks(coarse_two, BAND_ROWS // 2)
    blocks_four = band_blocks(coarse_four, BAND_ROWS // 4)
    lon_count = lax.axis_size("lon")
    lat_count = lax.axis_size("lat")
    devices = lon_count * lat_count
    capacity = max(2, 2 * blocks_two.shape[0] // devices)
    owners = owner_map[:, 0]
    onehot = (owners[:, None] == jnp.arange(devices, dtype=jnp.int32)[None, :]).astype(jnp.int32)
    rank_in = jnp.sum((jnp.cumsum(onehot, axis=0) - onehot) * onehot, axis=1)
    slot_index = owners * capacity + rank_in
    placing = (
        slot_index[:, None] == jnp.arange(devices * capacity, dtype=jnp.int32)[None, :]
    ).astype(jnp.float32)
    contract = (((0,), (0,)), ((), ()))
    send_two = lax.dot_general(
        placing,
        blocks_two,
        contract,
        precision=lax.Precision.HIGHEST,
        preferred_element_type=jnp.float32,
    )
    send_four = lax.dot_general(
        placing,
        blocks_four,
        contract,
        precision=lax.Precision.HIGHEST,
        preferred_element_type=jnp.float32,
    )
    received_two, received_four = (
        lax.all_to_all(send_two, ("lon", "lat"), split_axis=0, concat_axis=0, tiled=True),
        lax.all_to_all(send_four, ("lon", "lat"), split_axis=0, concat_axis=0, tiled=True),
    )
    return (updated, received_two[None], received_four[None])


def solution(mesh):
    in_specs = (
        P(None, None, "lat", "lon"),
        P(None, "lat", "lon"),
        P(None, "lat", "lon"),
        P(None, "lat", "lon"),
        P(None, "lat", "lon"),
        P(),
        P("lat", "lon"),
        P(("lon", "lat"), None),
    )
    out_specs = (
        P(None, None, "lat", "lon"),
        P(("lon", "lat"), None, None),
        P(("lon", "lat"), None, None),
    )
    return jax.shard_map(local, mesh=mesh, in_specs=in_specs, out_specs=out_specs, check_vma=False)
```

profile of v0, /device:TPU:0, one launch (start us, length us, event | category | flops | bytes accessed | tf_op | source)
XLA Modules:
  0.0 290.8 jit_solution(1426492618948505329)
XLA Ops:
  5.3 2.6 copy.122
  13.5 3.0 %collective-permute-start.2 = (f32[6,16,1,128]{3,1,2,0:T(8,128)}, f32[6,16,1,128]{3,1,2,0:T(8,128)}, u32[]{:S(2)}, u32[]{:S(2)}) collective-permute-start(f32[6,16,1,128]{3,1,2,0:T(8,128)} %get-tuple-element.32), channel_id=1, source_target_pairs={{0,1},{1,2},{2,3},{3,4},{4,5},{5,6},{6,7},{8,9},{9,10},{10,11},{11... | collective-permute-start | bytes 147464 | tf_op jit(solution)/shard_map/ppermute | solution.py:21
  20.1 8.2 %fusion.20 = (f32[4,16,128,1]{3,2,1,0:T(8,128)}, f32[4,16,128,1]{3,2,1,0:T(8,128)}) fusion(f32[4,16,128,128]{3,2,1,0:T(8,128)} %param.8), kind=kLoop, calls=%fused_computation.67 | loop fusion | bytes 131072 | tf_op jit(solution)/shard_map/slice | solution.py:76
  30.0 3.2 %copy.162 = f32[4,16,128,1]{2,1,3,0:T(8,128)S(1)} copy(f32[4,16,128,1]{3,2,1,0:T(8,128)} %get-tuple-element.9) | data formatting | bytes 65536
  33.3 2.8 copy.163
  36.8 2.9 %collective-permute-start.1 = (f32[6,16,128,1]{2,1,3,0:T(8,128)}, f32[6,16,128,1]{2,1,3,0:T(8,128)}, u32[]{:S(2)}, u32[]{:S(2)}) collective-permute-start(f32[6,16,128,1]{2,1,3,0:T(8,128)} %get-tuple-element.31), channel_id=1, source_target_pairs={{8,0},{16,8},{24,16},{0,24},{9,1},{17,9},{25,17},{1,25},{10,2},{18... | collective-permute-start | bytes 147464 | tf_op jit(solution)/shard_map/ppermute | solution.py:24
  40.8 7.5 %copy.156 = f32[16,128,128]{0,2,1:T(8,128)} copy(f32[16,128,128]{1,0,2:T(8,128)S(1)} %get-tuple-element.5) | data formatting | bytes 2097152 | tf_op jit(solution)/shard_map/mul | solution.py:161
  48.3 9.6 %reduce_sum.55 = f32[16,64,64]{0,2,1:T(8,128)S(1)} reduce(f32[16,64,2,64,2]{0,4,3,2,1:T(2,128)} %bitcast.102, f32[]{:T(128)} %constant.32.clone.1), dimensions={2,4}, to_apply=%region_3.4 | reduce | flops 196608 | bytes 1310724 | tf_op jit(solution)/shard_map/reduce_sum | solution.py:51
  57.9 2.8 reduce_sum.58
  64.8 2.6 copy.146
  68.5 2.6 copy.153
  72.4 5.4 %slice.139 = f32[4,16,128,127]{3,2,1,0:T(8,128)} slice(f32[4,16,128,128]{3,2,1,0:T(8,128)} %param.8), slice={[0:4], [0:16], [0:128], [1:128]} | slice | bytes 8323072 | tf_op jit(solution)/shard_map/slice | solution.py:84
  77.8 2.6 slice.157
  85.5 3.1 %broadcast_multiply_fusion.3 = (f32[16,128,128]{1,0,2:T(8,128)}, f32[16,128,128]{1,0,2:T(8,128)}) fusion(f32[16,128,128]{1,0,2:T(8,128)} %copy-done.2, f32[16,128,1]{1,0,2:T(8,128)S(1)} %get-tuple-element.39, f32[16,128,127]{1,0,2:T(8,128)} %slice.171), kind=kLoop, calls=%fused_computation.25 | loop fusion | flops 1572864 | bytes 4194304 | tf_op jit(solution)/shard_map/mul | solution.py:43
  93.9 2.6 copy.129
  96.5 2.6 copy.131
  99.8 2.7 copy.130
  102.5 2.6 copy.132
  109.7 3.6 %broadcast_multiply_fusion.2 = (f32[16,128,128]{1,0,2:T(8,128)}, f32[16,128,128]{1,0,2:T(8,128)}) fusion(f32[16,128,128]{1,0,2:T(8,128)} %copy.146, f32[16,1,128]{1,0,2:T(8,128)} %copy.145, f32[16,127,128]{1,0,2:T(8,128)} %slice.184), kind=kLoop, calls=%fused_computation.24 | loop fusion | flops 1572864 | bytes 4194304 | tf_op jit(solution)/shard_map/mul | solution.py:43
  115.8 2.6 copy.149
  118.4 3.9 %maximum_minimum_fusion = (f32[16,128,128]{1,0,2:T(8,128)}, f32[16,128,128]{1,0,2:T(8,128)}, f32[16,128,128]{1,0,2:T(8,128)}) fusion(f32[16,128,128]{1,0,2:T(8,128)S(1)} %get-tuple-element.6, f32[16,128,1]{1,0,2:T(8,128)S(1)} %copy-done.12, f32[16,128,127]{1,0,2:T(8,128)} %slice.168, f32[128,128]{0,1:T(8,128)S(1)} %copy.151, f32[16,1,128]{1,0,2:T(8,128)} %copy.142, ...), kind=kLoop, calls=%fused_computation.13 | loop fusion | flops 1572864 | bytes 6356992 | tf_op jit(solution)/shard_map/min | solution.py:40
  122.3 2.6 copy.126
  128.9 9.2 %subtract_multiply_fusion.1 = (f32[4,16,128,128]{3,2,1,0:T(8,128)S(1)}, f32[4,16,128,128]{3,2,1,0:T(8,128)S(1)}) fusion(f32[4,16,128,128]{3,2,1,0:T(8,128)} %param.8, f32[4,16,128,1]{3,2,1,0:T(8,128)} %copy.130, f32[4,16,128,127]{3,2,1,0:T(8,128)} %slice.139, f32[16]{0:T(128)S(1)} %copy-done.14, f32[16,128,128]{2,1,0:T(8,128)} %copy.131, ...), kind=kLoop, calls=%fused_computation.9 | loop fusion | flops 18874368 | bytes 27263040 | tf_op jit(solution)/shard_map/mul | solution.py:42
  138.3 6.7 %broadcast_multiply_fusion = (f32[4,16,128,128]{3,2,1,0:T(8,128)}, f32[4,16,128,128]{3,2,1,0:T(8,128)}) fusion(f32[16,128,128]{2,1,0:T(8,128)S(1)} %copy-done.4, f32[4,16,128,128]{3,2,1,0:T(8,128)S(1)} %copy-done.1, f32[16,128,128]{2,1,0:T(8,128)S(1)} %copy-done.5, f32[4,16,128,128]{3,2,1,0:T(8,128)S(1)} %get-tuple-element.8, ...), kind=kLoop, calls=%fused_computation.12 | loop fusion | flops 9437184 | bytes 31457280 | tf_op jit(solution)/shard_map/mul | solution.py:57
  145.1 18.3 %copy.154 = f32[4,16,128,128]{1,3,2,0:T(8,128)} copy(f32[4,16,128,128]{3,2,1,0:T(8,128)} %get-tuple-element.3) | data formatting | bytes 8388608 | tf_op jit(solution)/shard_map/mul | solution.py:57
  163.4 33.4 %reduce_sum.53 = f32[4,16,64,64]{1,3,2,0:T(8,128)} reduce(f32[4,16,64,2,64,2]{1,5,4,3,2,0:T(2,128)} %bitcast.98, f32[]{:T(128)} %constant.32.clone.1), dimensions={3,5}, to_apply=%region_2.3 | reduce | flops 786432 | bytes 5242884 | tf_op jit(solution)/shard_map/reduce_sum | solution.py:51
  196.8 10.9 %reduce_sum.56 = f32[4,16,32,32]{1,3,2,0:T(8,128)} reduce(f32[4,16,32,2,32,2]{1,5,4,3,2,0:T(2,128)} %bitcast.99, f32[]{:T(128)} %constant.32.clone.1), dimensions={3,5}, to_apply=%region_4.5 | reduce | flops 196608 | bytes 1310724 | tf_op jit(solution)/shard_map/reduce_sum | solution.py:51
  212.6 5.8 %all-to-all-start.1 = ((f32[32,8,512]{2,1,0:T(8,128)}), f32[32,8,512]{2,1,0:T(8,128)}, u32[]{:S(2)}, u32[]{:S(2)}) async-start(f32[32,8,512]{2,1,0:T(8,128)} %fusion.5), calls=%async_computation.1 | async-start | bytes 1048576 | tf_op jit(solution)/shard_map/all_to_all | solution.py:192
  222.2 5.5 %copy.155 = f32[4,16,64,64]{3,2,1,0:T(8,128)S(1)} copy(f32[4,16,64,64]{1,3,2,0:T(8,128)} %reduce_sum.53) | data formatting | bytes 2097152 | tf_op jit(solution)/shard_map/reduce_sum | solution.py:51
  231.3 3.4 %all-to-all-done.1 = f32[32,8,512]{2,1,0:T(8,128)} async-done(((f32[32,8,512]{2,1,0:T(8,128)}), f32[32,8,512]{2,1,0:T(8,128)}, u32[]{:S(2)}, u32[]{:S(2)}) %all-to-all-start.1) | async-done | bytes 524320 | tf_op jit(solution)/shard_map/all_to_all | solution.py:192
  234.7 2.7 all-to-all-start
  237.5 50.1 %all-to-all-done = f32[32,8,2048]{2,1,0:T(8,128)S(1)} async-done(((f32[32,8,2048]{2,1,0:T(8,128)}), f32[32,8,2048]{2,1,0:T(8,128)S(1)}, u32[]{:S(2)}, u32[]{:S(2)}) %all-to-all-start) | async-done | bytes 2097184 | tf_op jit(solution)/shard_map/all_to_all | solution.py:191
  (100 shorter events, 61.5 us)
Async XLA Ops:
  1.5 11.2 %copy-start.10 = (f32[16,1,128]{2,1,0:T(1,128)}, f32[16,1,128]{2,1,0:T(1,128)S(1)}, u32[]{:S(2)}) copy-start(f32[16,1,128]{2,1,0:T(1,128)S(1)} %get-tuple-element.28) | copy-start | bytes 24580
  9.3 31.5 %copy-start.3 = (f32[16,128,128]{1,0,2:T(8,128)}, f32[16,128,128]{1,0,2:T(8,128)S(1)}, u32[]{:S(2)}) copy-start(f32[16,128,128]{1,0,2:T(8,128)S(1)} %get-tuple-element.5) | copy-start | bytes 3145732
  12.3 0.6 copy-start.8
  13.5 77.3 %collective-permute-start.2 = (f32[6,16,1,128]{3,1,2,0:T(8,128)}, f32[6,16,1,128]{3,1,2,0:T(8,128)}, u32[]{:S(2)}, u32[]{:S(2)}) collective-permute-start(f32[6,16,1,128]{3,1,2,0:T(8,128)} %get-tuple-element.32), channel_id=1, source_target_pairs={{0,1},{1,2},{2,3},{3,4},{4,5},{5,6},{6,7},{8,9},{9,10},{10,11},{11... | collective-permute-start | bytes 147464 | tf_op jit(solution)/shard_map/ppermute | solution.py:21
  16.5 72.1 %collective-permute-start.3 = (f32[6,16,128]{2,1,0:T(8,128)}, f32[6,16,128]{2,1,0:T(8,128)}, u32[]{:S(2)}, u32[]{:S(2)}) collective-permute-start(f32[6,16,128]{2,1,0:T(8,128)} %get-tuple-element.33), channel_id=1, source_target_pairs={{0,8},{8,0},{16,24},{24,16},{1,9},{9,1},{17,25},{25,17},{2,10},{10... | collective-permute-start | bytes 147464 | tf_op jit(solution)/shard_map/ppermute | solution.py:36
  18.8 87.2 %collective-permute-start.5 = (f32[6,16,1,128]{3,1,2,0:T(8,128)}, f32[6,16,1,128]{3,1,2,0:T(8,128)}, u32[]{:S(2)}, u32[]{:S(2)}) collective-permute-start(f32[6,16,1,128]{3,1,2,0:T(8,128)} %get-tuple-element.34), channel_id=1, source_target_pairs={{1,0},{2,1},{3,2},{4,3},{5,4},{6,5},{7,6},{9,8},{10,9},{11,10},{12... | collective-permute-start | bytes 147464 | tf_op jit(solution)/shard_map/ppermute | solution.py:24
  30.0 6.1 %copy-start.2 = (f32[16,128,128]{1,0,2:T(8,128)}, f32[16,128,128]{1,0,2:T(8,128)S(1)}, u32[]{:S(2)}) copy-start(f32[16,128,128]{1,0,2:T(8,128)S(1)} %copy.124) | copy-start | bytes 3145732
  30.0 9.7 %copy-start.15 = (s32[128,1]{0,1:T(1,128)S(1)}, s32[128,1]{0,1:T(1,128)}, u32[]{:S(2)}) copy-start(s32[128,1]{0,1:T(1,128)} %param.15) | copy-start | bytes 1540
  36.8 53.3 %collective-permute-start = (f32[6,16,128,1]{2,1,3,0:T(8,128)}, f32[6,16,128,1]{2,1,3,0:T(8,128)}, u32[]{:S(2)}, u32[]{:S(2)}) collective-permute-start(f32[6,16,128,1]{2,1,3,0:T(8,128)} %get-tuple-element.30), channel_id=1, source_target_pairs={{0,8},{8,16},{16,24},{24,0},{1,9},{9,17},{17,25},{25,1},{2,10},{10... | collective-permute-start | bytes 147464 | tf_op jit(solution)/shard_map/ppermute | solution.py:21
  36.8 47.4 %collective-permute-start.1 = (f32[6,16,128,1]{2,1,3,0:T(8,128)}, f32[6,16,128,1]{2,1,3,0:T(8,128)}, u32[]{:S(2)}, u32[]{:S(2)}) collective-permute-start(f32[6,16,128,1]{2,1,3,0:T(8,128)} %get-tuple-element.31), channel_id=1, source_target_pairs={{8,0},{16,8},{24,16},{0,24},{9,1},{17,9},{25,17},{1,25},{10,2},{18... | collective-permute-start | bytes 147464 | tf_op jit(solution)/shard_map/ppermute | solution.py:24
  72.4 5.4 %copy-start = (f32[4,16,128,128]{3,2,1,0:T(8,128)S(1)}, f32[4,16,128,128]{3,2,1,0:T(8,128)}, u32[]{:S(2)}) copy-start(f32[4,16,128,128]{3,2,1,0:T(8,128)} %param.8) | copy-start | bytes 12582916
  84.2 6.7 %copy-start.9 = (f32[16,1,128]{2,0,1:T(8,128)S(1)}, f32[16,1,128]{2,0,1:T(8,128)}, u32[]{:S(2)}) copy-start(f32[16,1,128]{2,0,1:T(8,128)} %copy-done.8) | copy-start | bytes 24580
  84.2 6.7 %copy-start.11 = (f32[16,1,128]{2,1,0:T(1,128)S(1)}, f32[16,1,128]{2,1,0:T(1,128)}, u32[]{:S(2)}) copy-start(f32[16,1,128]{2,1,0:T(1,128)} %copy-done.10) | copy-start | bytes 24580
  84.2 7.4 %copy-start.13 = (f32[16]{0:T(128)S(1)}, f32[16]{0:T(128)}, u32[]{:S(2)}) copy-start(f32[16]{0:T(128)} %param.13) | copy-start | bytes 196
  88.6 16.5 %collective-permute-start.4 = (f32[6,16,128]{2,1,0:T(8,128)}, f32[6,16,128]{2,1,0:T(8,128)}, u32[]{:S(2)}, u32[]{:S(2)}) collective-permute-start(f32[6,16,128]{2,1,0:T(8,128)} %collective-permute-done.3), channel_id=1, source_target_pairs={{0,16},{16,0},{8,24},{24,8},{1,17},{17,1},{9,25},{25,9},{2,18},{18... | collective-permute-start | bytes 147464 | tf_op jit(solution)/shard_map/ppermute | solution.py:36
  109.7 8.7 %copy-start.12 = (f32[16,128,1]{1,0,2:T(8,128)S(1)}, f32[16,128,1]{1,0,2:T(8,128)}, u32[]{:S(2)}) copy-start(f32[16,128,1]{1,0,2:T(8,128)} %get-tuple-element.38) | copy-start | bytes 24580
  122.3 5.2 %copy-start.6 = (f32[16,128,128]{1,0,2:T(8,128)S(1)}, f32[16,128,128]{1,0,2:T(8,128)}, u32[]{:S(2)}) copy-start(f32[16,128,128]{1,0,2:T(8,128)} %get-tuple-element.21) | copy-start | bytes 3145732
  122.3 6.6 %copy-start.14 = (f32[16]{0:T(128)S(1)}, f32[16]{0:T(128)}, u32[]{:S(2)}) copy-start(f32[16]{0:T(128)} %param.13) | copy-start | bytes 196
  128.9 9.3 %copy-start.1 = (f32[4,16,128,128]{3,2,1,0:T(8,128)S(1)}, f32[4,16,128,128]{3,2,1,0:T(8,128)}, u32[]{:S(2)}) copy-start(f32[4,16,128,128]{3,2,1,0:T(8,128)} %param.8) | copy-start | bytes 12582916
  128.9 9.3 %copy-start.4 = (f32[16,128,128]{2,1,0:T(8,128)S(1)}, f32[16,128,128]{2,1,0:T(8,128)}, u32[]{:S(2)}) copy-start(f32[16,128,128]{2,1,0:T(8,128)} %copy.153) | copy-start | bytes 3145732
  128.9 9.4 %copy-start.5 = (f32[16,128,128]{2,1,0:T(8,128)S(1)}, f32[16,128,128]{2,1,0:T(8,128)}, u32[]{:S(2)}) copy-start(f32[16,128,128]{2,1,0:T(8,128)} %copy.152) | copy-start | bytes 3145732
  128.9 9.4 %copy-start.7 = (f32[4,16,1,128]{3,1,2,0:T(8,128)S(1)}, f32[4,16,1,128]{3,1,2,0:T(8,128)}, u32[]{:S(2)}) copy-start(f32[4,16,1,128]{3,1,2,0:T(8,128)} %subtract_multiply_fusion.2) | copy-start | bytes 98308
  207.7 3.7 %copy-start.16 = (s32[128]{0:T(128)S(1)}, s32[128]{0:T(128)}, u32[]{:S(2)}) copy-start(s32[128]{0:T(128)} %fusion.18) | copy-start | bytes 1540
  212.6 22.1 %all-to-all-start.1 = ((f32[32,8,512]{2,1,0:T(8,128)}), f32[32,8,512]{2,1,0:T(8,128)}, u32[]{:S(2)}, u32[]{:S(2)}) async-start(f32[32,8,512]{2,1,0:T(8,128)} %fusion.5), calls=%async_computation.1 | async-start | bytes 1048576 | tf_op jit(solution)/shard_map/all_to_all | solution.py:192
  234.7 52.8 %all-to-all-start = ((f32[32,8,2048]{2,1,0:T(8,128)}), f32[32,8,2048]{2,1,0:T(8,128)S(1)}, u32[]{:S(2)}, u32[]{:S(2)}) async-start(f32[32,8,2048]{2,1,0:T(8,128)} %fusion.7), calls=%async_computation | async-start | bytes 4194304 | tf_op jit(solution)/shard_map/all_to_all | solution.py:191
where the time goes:
time: 293 us; the launch traced here: 291 us
  local copies, waits for them, and re-layouts  119 us (41%)
  other arithmetic  94 us (32%)
  waiting for transfers between devices  53.5 us (18%)
  starting transfers between devices  19.5 us (7%)
  matrix products  3.56 us (1%)
    reduce_sum x4, other arithmetic, pool_pairs(): field.reshape(old_shape[:-2] + (old_shape[-2] // 2, 2, old_shape[-1] // 2...  56.7 us
    all_to_all x1, waiting for transfers between devices, local(): lax.all_to_all(send_two, ('lon', 'lat'), split_axis=0, concat_axis=0, til...  50.1 us
    unnamed x43, local copies, waits for them, and re-layouts  19.2 us
    mul x1, local copies, waits for them, and re-layouts, coarsen(): weighted = pool_pairs(updated * weight[None])  18.3 us
    mul x3, other arithmetic, face_flux(): open_depth * (0.5 * face_speed * (lower_val + upper_val) - 0.5 * jnp.abs(...  11.5 us
    mul x2, local copies, waits for them, and re-layouts, local(): coarse_two, coarse_four = coarsen(updated, cell_area[None] * wet_depth)  10.1 us
    slice x3, local copies, waits for them, and re-layouts, shifted_east(): return jnp.concatenate([field[..., 1:], column[..., None]], axis=-1)  8.76 us
    slice x3, local copies, waits for them, and re-layouts, column_edges(): return jnp.concatenate([field[..., :1], field[..., -1:]], axis=-1)  8.16 us
  transfers between devices with their start and end apart: 8, of which 2 were waited for; matrix products, arithmetic and copies ran while one was open for 32% of the time, Pallas kernels for 0%

commit v1 on v0

v1 whole, which is shorter than its diff:
```python
import functools

import jax
import jax.numpy as jnp
from jax import lax
from jax.experimental import pallas as pl
from jax.experimental.pallas import tpu as pltpu
from jax.sharding import PartitionSpec as P

BAND_ROWS = 16
MESH = pl.DeviceIdType.MESH

time_step = 0.05
depth_floor = 0.25
weight_floor = 0.25


def pieces(x):
    high = x.astype(jnp.bfloat16)
    rest = x - high.astype(jnp.float32)
    middle = rest.astype(jnp.bfloat16)
    low = (rest - middle.astype(jnp.float32)).astype(jnp.bfloat16)
    return high, middle, low


def dot(a, b):
    return jnp.dot(a, b, preferred_element_type=jnp.float32)


def exact_dot(x, ones):
    high, middle, low = pieces(x)
    return (dot(low, ones) + dot(middle, ones)) + dot(high, ones)


def kernel(
    sizes,
    tracers,
    fill,
    mask,
    east,
    north,
    mixing,
    area,
    owner,
    updated_out,
    recv_out,
    updated,
    depth,
    product,
    blocks,
    send,
    pool_two,
    pool_four,
    col_pack,
    col_got,
    row_pack,
    row_got,
    halo_send,
    halo_recv,
    send_sem,
    recv_sem,
    out_sem,
):
    n_lon, n_lat, rows_each = sizes
    n = n_lon * n_lat
    nt, nl, nr, nc = tracers.shape
    lon = lax.axis_index("lon")
    lat = lax.axis_index("lat")
    me = lon * n_lat + lat

    barrier = pltpu.get_barrier_semaphore()

    def greet(j, carry):
        target = lax.rem(me + j, n)
        pl.semaphore_signal(
            barrier, inc=1, device_id=(target // n_lat, lax.rem(target, n_lat)), device_id_type=MESH
        )
        return carry

    lax.fori_loop(1, n, greet, 0)

    lane = lax.broadcasted_iota(jnp.int32, (nr, nc), 1)
    row = lax.broadcasted_iota(jnp.int32, (nr, nc), 0)

    def pack(k, carry):
        west, east_side = carry
        depth[k] = fill[k] * mask[k].astype(jnp.float32)
        for item in range(nt + 2):
            if item < nt:
                x = tracers[item, k]
            elif item == nt:
                x = depth[k]
            else:
                x = east[k]
            at = item * nl + k
            west = jnp.where(lane == at, x[:, 0:1], west)
            east_side = jnp.where(lane == at, x[:, nc - 1 : nc], east_side)
            y = north[k] if item == nt + 1 else x
            row_pack[0, pl.ds(at, 1), :] = y[0:1, :]
            row_pack[1, pl.ds(at, 1), :] = y[nr - 1 : nr, :]
        return west, east_side

    zero = jnp.zeros((nr, nc), jnp.float32)
    west, east_side = lax.fori_loop(0, nl, pack, (zero, zero))
    col_pack[0] = west
    col_pack[1] = east_side

    at_fold = lat == n_lat - 1
    items = row_pack.shape[1]

    @pl.when(at_fold)
    def _():
        flip = (
            lax.broadcasted_iota(jnp.int32, (nc, nc), 0)
            + lax.broadcasted_iota(jnp.int32, (nc, nc), 1)
            == nc - 1
        )
        turned = exact_dot(row_pack[1], flip.astype(jnp.float32).astype(jnp.bfloat16))
        index = lax.broadcasted_iota(jnp.int32, (items, nc), 0)
        row_pack[1] = jnp.where(index >= (nt + 1) * nl, -turned, turned)

    @pl.when(lat == 0)
    def _():
        row_got[0] = jnp.zeros((items, nc), jnp.float32)

    pl.semaphore_wait(barrier, n - 1)

    def halo(src, dst, at_send, at_recv, to_lon, to_lat):
        return pltpu.make_async_remote_copy(
            src_ref=src,
            dst_ref=dst,
            send_sem=halo_send.at[at_send],
            recv_sem=halo_recv.at[at_recv],
            device_id=(to_lon, to_lat),
            device_id_type=MESH,
        )

    lon_west = lax.rem(lon + n_lon - 1, n_lon)
    lon_east = lax.rem(lon + 1, n_lon)
    to_west = halo(col_pack.at[0], col_got.at[1], 0, 1, lon_west, lat)
    to_east = halo(col_pack.at[1], col_got.at[0], 1, 0, lon_east, lat)
    to_south = halo(row_pack.at[0], row_got.at[1], 2, 3, lon, lat - 1)
    to_north = halo(row_pack.at[1], row_got.at[0], 3, 2, lon, lat + 1)
    to_fold = halo(row_pack.at[1], row_got.at[1], 3, 3, n_lon - 1 - lon, lat)
    to_west.start()
    to_east.start()

    @pl.when(lat > 0)
    def _():
        to_south.start()

    @pl.when(at_fold)
    def _():
        to_fold.start()

    @pl.when(jnp.logical_not(at_fold))
    def _():
        to_north.start()

    def matrix(shape, shift):
        hit = (lax.broadcasted_iota(jnp.int32, shape, 0) >> shift) == lax.broadcasted_iota(
            jnp.int32, shape, 1
        )
        return hit.astype(jnp.float32).astype(jnp.bfloat16)

    pool_two[...] = matrix(pool_two.shape, 1)
    pool_four[...] = matrix(pool_four.shape, 2)

    to_west.wait()
    to_east.wait()

    @pl.when(lat > 0)
    def _():
        to_south.wait_send()
        to_north.wait_recv()

    @pl.when(at_fold)
    def _():
        to_fold.wait()

    @pl.when(jnp.logical_not(at_fold))
    def _():
        to_north.wait_send()
        to_south.wait_recv()

    bands = nr // BAND_ROWS
    quads = BAND_ROWS // 4

    def level_out(k):
        return pltpu.make_async_copy(updated.at[:, k], updated_out.at[:, k], out_sem.at[k])

    def level(k, carry):
        def around(x, item):
            at = item * nl + k
            x_east = jnp.where(
                lane == nc - 1,
                pltpu.roll(col_got[1], nc - 1 - at, 1),
                pltpu.roll(x, nc - 1, 1),
            )
            x_west = jnp.where(
                lane == 0, pltpu.roll(col_got[0], nc - at, 1), pltpu.roll(x, 1, 1)
            )
            return x_east, x_west

        def along(x, item):
            at = item * nl + k
            x_north = jnp.where(
                row == nr - 1, row_got[1, pl.ds(at, 1), :], pltpu.roll(x, nr - 1, 0)
            )
            x_south = jnp.where(row == 0, row_got[0, pl.ds(at, 1), :], pltpu.roll(x, 1, 0))
            return x_north, x_south

        kappa = mixing[k]
        h = depth[k]
        u = east[k]
        v = north[k]
        grid_area = area[...]
        gain = time_step / (grid_area * jnp.maximum(h, depth_floor))
        h_east, h_west = around(h, nt)
        h_north, h_south = along(h, nt)
        u_east, u_west = around(u, nt + 1)
        v_north, v_south = along(v, nt + 1)

        def face(h_other, a, b):
            speed = 0.5 * (a + b)
            scaled = gain * jnp.minimum(h, h_other)
            return (
                scaled * (jnp.maximum(speed, 0.0) + kappa),
                scaled * (kappa - jnp.minimum(speed, 0.0)),
            )

        out_e, in_e = face(h_east, u, u_east)
        in_w, out_w = face(h_west, u_west, u)
        out_n, in_n = face(h_north, v, v_north)
        in_s, out_s = face(h_south, v_south, v)
        loss = (out_e + out_w) + (out_n + out_s)
        weight = grid_area * h
        product[nt] = weight
        for t in range(nt):
            x = tracers[t, k]
            x_east, x_west = around(x, t)
            x_north, x_south = along(x, t)
            change = (in_w * x_west + in_e * x_east) + (in_s * x_south + in_n * x_north)
            new = x + (change - loss * x)
            updated[t, k] = new
            product[t] = new * weight
        level_out(k).start()

        upper, lower, whole = [], [], []
        for t in range(nt + 1):
            both = []
            for i in range(quads):
                four = [
                    product[t, pl.ds(4 * i + j, bands, stride=BAND_ROWS), :] for j in range(4)
                ]
                upper.append(four[0] + four[1])
                lower.append(four[2] + four[3])
                both.append(upper[-1] + lower[-1])
            whole.append(jnp.concatenate(both, axis=1))
        two = exact_dot(
            jnp.concatenate(
                [jnp.concatenate(upper, axis=0), jnp.concatenate(lower, axis=0)], axis=1
            ),
            pool_two[...],
        )
        four = exact_dot(jnp.concatenate(whole, axis=0), pool_four[...])
        at_rows = pl.ds(pl.multiple_of(k * bands, bands), bands)
        span = quads * bands
        den_two = jnp.maximum(two[nt * span :], weight_floor)
        den_four = jnp.maximum(four[nt * bands :], weight_floor)
        for t in range(nt):
            ratio = two[t * span : (t + 1) * span] / den_two
            for i in range(quads):
                column = (t * quads + i) * nc
                blocks[at_rows, column : column + nc] = ratio[i * bands : (i + 1) * bands]
            column = (nt * quads + t) * nc
            blocks[at_rows, column : column + nc] = four[t * bands : (t + 1) * bands] / den_four
        return carry

    lax.fori_loop(0, nl, level, 0)

    units = blocks.shape[0]
    unit_a = lax.broadcasted_iota(jnp.int32, (units, units), 0)
    unit_b = lax.broadcasted_iota(jnp.int32, (units, units), 1)
    own_col = jnp.broadcast_to(owner[...], (units, units))
    own_row = jnp.sum(jnp.where(unit_a == unit_b, own_col, 0), axis=0, keepdims=True)
    earlier = jnp.logical_and(own_col == own_row, unit_a < unit_b)
    rank = jnp.sum(jnp.where(earlier, 1, 0), axis=0, keepdims=True)
    slot = own_row * rows_each + rank
    place = (
        (lax.broadcasted_iota(jnp.int32, (n * rows_each, units), 0) == slot)
        .astype(jnp.float32)
        .astype(jnp.bfloat16)
    )
    place = jnp.concatenate([place, place, place], axis=1)
    width = blocks.shape[1]
    chunk = 4 * nc
    for start in range(0, width, chunk):
        stop = min(width, start + chunk)
        send[:, start:stop] = dot(
            place, jnp.concatenate(pieces(blocks[:, start:stop]), axis=0)
        )

    mine = pl.ds(pl.multiple_of(me * rows_each, rows_each), rows_each)

    def to_peer(j):
        target = lax.rem(me + j, n)
        theirs = pl.ds(pl.multiple_of(target * rows_each, rows_each), rows_each)
        return pltpu.make_async_remote_copy(
            src_ref=send.at[theirs, :],
            dst_ref=recv_out.at[mine, :],
            send_sem=send_sem.at[j],
            recv_sem=recv_sem.at[j],
            device_id=(target // n_lat, lax.rem(target, n_lat)),
            device_id_type=MESH,
        )

    def begin(j, carry):
        to_peer(j).start()
        return carry

    lax.fori_loop(1, n, begin, 0)
    own_copy = pltpu.make_async_copy(send.at[mine, :], recv_out.at[mine, :], send_sem.at[0])
    own_copy.start()

    def end_level(k, carry):
        level_out(k).wait()
        return carry

    lax.fori_loop(0, nl, end_level, 0)
    own_copy.wait()

    def end(j, carry):
        source = lax.rem(me + n - j, n)
        theirs = pl.ds(pl.multiple_of(source * rows_each, rows_each), rows_each)
        copy = to_peer(j)
        copy.wait_send()
        pltpu.make_async_remote_copy(
            src_ref=send.at[mine, :],
            dst_ref=recv_out.at[theirs, :],
            send_sem=send_sem.at[j],
            recv_sem=recv_sem.at[j],
            device_id=(source // n_lat, lax.rem(source, n_lat)),
            device_id_type=MESH,
        ).wait_recv()
        return carry

    lax.fori_loop(1, n, end, 0)


def local(
    tracers, fill_fraction, ocean_mask, east_speed, north_speed, diffusivity, cell_area, owner_map
):
    nt, nl, nr, nc = tracers.shape
    n_lon = lax.axis_size("lon")
    n_lat = lax.axis_size("lat")
    n = n_lon * n_lat
    units = owner_map.shape[0]
    capacity = max(2, 2 * units // n)
    rows_each = -(-capacity // 8) * 8
    wide_two = nt * BAND_ROWS * nc // 4
    wide_four = nt * BAND_ROWS * nc // 16
    wide = wide_two + wide_four
    items = (nt + 2) * nl
    f32 = jnp.float32
    vmem = pl.BlockSpec(memory_space=pltpu.VMEM)
    updated, received = pl.pallas_call(
        functools.partial(kernel, (n_lon, n_lat, rows_each)),
        out_shape=(
            jax.ShapeDtypeStruct(tracers.shape, f32),
            jax.ShapeDtypeStruct((n * rows_each, wide), f32),
        ),
        in_specs=[vmem] * 5 + [pl.BlockSpec(memory_space=pltpu.SMEM)] + [vmem] * 2,
        out_specs=(pl.BlockSpec(memory_space=pl.ANY), pl.BlockSpec(memory_space=pl.ANY)),
        scratch_shapes=[
            pltpu.VMEM(tracers.shape, f32),
            pltpu.VMEM((nl, nr, nc), f32),
            pltpu.VMEM((nt + 1, nr, nc), f32),
            pltpu.VMEM((units, wide), f32),
            pltpu.VMEM((n * rows_each, wide), f32),
            pltpu.VMEM((2 * nc, nc), jnp.bfloat16),
            pltpu.VMEM((4 * nc, nc), jnp.bfloat16),
            pltpu.VMEM((2, nr, nc), f32),
            pltpu.VMEM((2, nr, nc), f32),
            pltpu.VMEM((2, items, nc), f32),
            pltpu.VMEM((2, items, nc), f32),
            pltpu.SemaphoreType.DMA((4,)),
            pltpu.SemaphoreType.DMA((4,)),
            pltpu.SemaphoreType.DMA((n,)),
            pltpu.SemaphoreType.DMA((n,)),
            pltpu.SemaphoreType.DMA((nl,)),
        ],
        compiler_params=pltpu.CompilerParams(
            collective_id=0, has_side_effects=True, vmem_limit_bytes=48 * 1024 * 1024
        ),
        name="substep",
    )(
        tracers,
        fill_fraction,
        ocean_mask,
        east_speed,
        north_speed,
        diffusivity,
        cell_area,
        owner_map,
    )
    if rows_each != capacity:
        received = received.reshape(n, rows_each, wide)[:, :capacity].reshape(n * capacity, wide)
    return updated, received[None, :, :wide_two], received[None, :, wide_two:]


def solution(mesh):
    in_specs = (
        P(None, None, "lat", "lon"),
        P(None, "lat", "lon"),
        P(None, "lat", "lon"),
        P(None, "lat", "lon"),
        P(None, "lat", "lon"),
        P(),
        P("lat", "lon"),
        P(("lon", "lat"), None),
    )
    out_specs = (
        P(None, None, "lat", "lon"),
        P(("lon", "lat"), None, None),
        P(("lon", "lat"), None, None),
    )
    return jax.shard_map(local, mesh=mesh, in_specs=in_specs, out_specs=out_specs, check_vma=False)
```

time: 293 us -> 103 us (0.35)
  local copies, waits for them, and re-layouts: 119 us -> 14.3 us
  other arithmetic: 94 us -> 0 us
  Pallas kernels: 0 us -> 86.3 us
  waiting for transfers between devices: 53.5 us -> 0 us
  starting transfers between devices: 19.5 us -> 0 us
  matrix products: 3.56 us -> 0 us
    pallas_call x0 -> x1, Pallas kernels: none -> 86.3 us  [local(): pl.pallas_call(functools.partial(kernel, (n_lon, n_lat, rows_each)), out_...]
    reduce_sum x5 -> x0, other arithmetic: 56.8 us -> none  [the longest x4 56.7 us: pool_pairs(): field.reshape(old_shape[:-2] + (old_shape[-2] // 2, 2, old_shape[-1] // 2...]
    all_to_all x2 -> x0, waiting for transfers between devices: 53.5 us -> none  [the longest x1 50.1 us: local(): lax.all_to_all(send_two, ('lon', 'lat'), split_axis=0, concat_axis=0, til...]
    mul x9 -> x0, local copies, waits for them, and re-layouts: 43.9 us -> none  [the longest x1 18.3 us: coarsen(): weighted = pool_pairs(updated * weight[None])]
    slice x19 -> x0, local copies, waits for them, and re-layouts: 33.5 us -> none  [the longest x3 8.76 us: shifted_east(): return jnp.concatenate([field[..., 1:], column[..., None]], axis=-1)]
    mul x9 -> x0, other arithmetic: 27.8 us -> none  [the longest x3 11.5 us: face_flux(): open_depth * (0.5 * face_speed * (lower_val + upper_val) - 0.5 * jnp.abs(...]
    ppermute x6 -> x0, starting transfers between devices: 11 us -> none  [the longest x2 4.2 us: padded(): lax.ppermute(lax.slice_in_dim(block, 0, width, axis=dim), axis, backward)]
    unnamed x43 -> x16, local copies, waits for them, and re-layouts: 19.2 us -> 9.17 us
  transfers between devices with their start and end apart: 8 -> 0, of which waited for: 2 -> 0; matrix products, arithmetic and copies ran while one was open for 32% -> 0% of each run, Pallas kernels for 0% -> 0%
where the time goes in v1:
time: 103 us; the launch traced here: 101 us
  Pallas kernels  86.3 us (84%)
  local copies, waits for them, and re-layouts  14.3 us (14%)
    pallas_call x1, Pallas kernels, local(): pl.pallas_call(functools.partial(kernel, (n_lon, n_lat, rows_each)), out_...  86.3 us
    unnamed x16, local copies, waits for them, and re-layouts  9.17 us
    broadcast_in_dim x2, local copies, waits for them, and re-layouts, local(): return (updated, received[None, :, :wide_two], received[None, :, wide_two:])  5.15 us

profile of v1, /device:TPU:0, one launch (start us, length us, event | category | flops | bytes accessed | tf_op | source)
XLA Modules:
  0.0 101.2 jit_solution(18235490940667660865)
XLA Ops:
  0.6 0.8 copy.11.owner
  1.4 0.0 copy-start
  1.4 1.2 %copy-done = f32[16,128,128]{2,1,0:T(8,128)S(1)} copy-done((f32[16,128,128]{2,1,0:T(8,128)S(1)}, f32[16,128,128]{2,1,0:T(8,128)}, u32[]{:S(2)}) %copy-start) | copy-done | bytes 1048600
  2.6 0.0 copy-start.1
  2.6 1.2 %copy-done.1 = s32[16,128,128]{2,1,0:T(8,128)S(1)} copy-done((s32[16,128,128]{2,1,0:T(8,128)S(1)}, s32[16,128,128]{2,1,0:T(8,128)}, u32[]{:S(2)}) %copy-start.1) | copy-done | bytes 1048600
  3.8 0.0 copy-start.2
  3.8 1.2 %copy-done.2 = f32[16,128,128]{2,1,0:T(8,128)S(1)} copy-done((f32[16,128,128]{2,1,0:T(8,128)S(1)}, f32[16,128,128]{2,1,0:T(8,128)}, u32[]{:S(2)}) %copy-start.2) | copy-done | bytes 1048600
  5.1 0.0 copy-start.3
  5.1 1.2 %copy-done.3 = f32[16,128,128]{2,1,0:T(8,128)S(1)} copy-done((f32[16,128,128]{2,1,0:T(8,128)S(1)}, f32[16,128,128]{2,1,0:T(8,128)}, u32[]{:S(2)}) %copy-start.3) | copy-done | bytes 1048600
  6.3 0.0 copy-start.4
  6.3 0.8 copy-done.4
  7.1 0.0 copy-start.5
  7.1 0.7 copy-done.5
  7.8 86.3 %substep.1 = (f32[4,16,128,128]{3,2,1,0:T(8,128)}, f32[256,2560]{1,0:T(8,128)}) custom-call(f32[4,16,128,128]{3,2,1,0:T(8,128)} %tracers.1, f32[16,128,128]{2,1,0:T(8,128)S(1)} %copy-done, s32[16,128,128]{2,1,0:T(8,128)S(1)} %copy-done.1, f32[16,128,128]{2,1,0:T(8,128)S(1)} %copy-done.2, f32[16,128,128]{2,1,0:T(8,128)S(1)} %copy-done.3, f32[16]{0:T(128)S(1)} %copy-done.5, ...), custom_call_target="tpu_custom_call" | custom-call | tf_op jit(solution)/shard_map/substep/pallas_call | solution.py:367
  94.1 0.0 copy-start.6
  94.1 2.0 %slice_bitcast_fusion.1 = f32[1,256,512]{2,1,0:T(8,128)} fusion(f32[256,2560]{1,0:T(8,128)} %get-tuple-element.6), kind=kLoop, calls=%fused_computation.1 | loop fusion | bytes 1048576 | tf_op jit(solution)/shard_map/broadcast_in_dim | solution.py:409
  96.1 3.1 %slice_bitcast_fusion = f32[1,256,2048]{2,1,0:T(8,128)} fusion(f32[256,2560]{1,0:T(8,128)} %get-tuple-element.6), kind=kLoop, calls=%fused_computation | loop fusion | bytes 4194304 | tf_op jit(solution)/shard_map/broadcast_in_dim | solution.py:409
  99.2 0.0 copy-done.6
  99.2 2.0 %copy.13 = f32[4,16,128,128]{3,2,1,0:T(8,128)} copy(f32[4,16,128,128]{3,2,1,0:T(8,128)S(1)} %copy-done.6) | data formatting | bytes 8388608
Async XLA Ops:
  1.4 1.2 %copy-start = (f32[16,128,128]{2,1,0:T(8,128)S(1)}, f32[16,128,128]{2,1,0:T(8,128)}, u32[]{:S(2)}) copy-start(f32[16,128,128]{2,1,0:T(8,128)} %fill.1) | copy-start | bytes 3145732
  2.6 1.2 %copy-start.1 = (s32[16,128,128]{2,1,0:T(8,128)S(1)}, s32[16,128,128]{2,1,0:T(8,128)}, u32[]{:S(2)}) copy-start(s32[16,128,128]{2,1,0:T(8,128)} %mask.1) | copy-start | bytes 3145732
  3.8 1.2 %copy-start.2 = (f32[16,128,128]{2,1,0:T(8,128)S(1)}, f32[16,128,128]{2,1,0:T(8,128)}, u32[]{:S(2)}) copy-start(f32[16,128,128]{2,1,0:T(8,128)} %east.1) | copy-start | bytes 3145732
  5.1 1.2 %copy-start.3 = (f32[16,128,128]{2,1,0:T(8,128)S(1)}, f32[16,128,128]{2,1,0:T(8,128)}, u32[]{:S(2)}) copy-start(f32[16,128,128]{2,1,0:T(8,128)} %north.1) | copy-start | bytes 3145732
  6.3 0.8 copy-start.4
  7.1 0.7 copy-start.5
  94.1 5.2 %copy-start.6 = (f32[4,16,128,128]{3,2,1,0:T(8,128)S(1)}, f32[4,16,128,128]{3,2,1,0:T(8,128)}, u32[]{:S(2)}) copy-start(f32[4,16,128,128]{3,2,1,0:T(8,128)} %get-tuple-element.10) | copy-start | bytes 12582916

commit v2 on v1

v2 whole, which is shorter than its diff:
```python
import functools

import jax
import jax.numpy as jnp
from jax import lax
from jax.experimental import pallas as pl
from jax.experimental.pallas import tpu as pltpu
from jax.sharding import PartitionSpec as P

BAND_ROWS = 16
MESH = pl.DeviceIdType.MESH

time_step = 0.05
depth_floor = 0.25
weight_floor = 0.25


def pieces(x):
    high = x.astype(jnp.bfloat16)
    rest = x - high.astype(jnp.float32)
    middle = rest.astype(jnp.bfloat16)
    low = (rest - middle.astype(jnp.float32)).astype(jnp.bfloat16)
    return high, middle, low


def dot(a, b):
    return jnp.dot(a, b, preferred_element_type=jnp.float32)


def exact_dot(x, ones):
    high, middle, low = pieces(x)
    return (dot(low, ones) + dot(middle, ones)) + dot(high, ones)


def kernel(
    sizes,
    tracers_in,
    fill_in,
    mask_in,
    east_in,
    north_in,
    mixing,
    area_in,
    owner_in,
    updated_out,
    two_out,
    four_out,
    tracers,
    depth,
    mask,
    east,
    north,
    area,
    owner,
    updated,
    coef,
    product,
    den_two,
    den_four,
    blocks,
    send_first,
    send_rest,
    send_four,
    place,
    pool_two,
    pool_four,
    col_pack,
    col_got,
    row_pack,
    row_got,
    halo_send,
    halo_recv,
    send_sem,
    recv_sem,
    out_sem,
    in_sem,
):
    n_lon, n_lat, rows_each = sizes
    n = n_lon * n_lat
    nt, nl, nr, nc = tracers.shape
    lon = lax.axis_index("lon")
    lat = lax.axis_index("lat")
    me = lon * n_lat + lat

    barrier = pltpu.get_barrier_semaphore()
    inputs = [
        pltpu.make_async_copy(source, held, in_sem.at[index])
        for index, (source, held) in enumerate(
            (
                (fill_in, depth),
                (mask_in, mask),
                (east_in, east),
                (north_in, north),
                (tracers_in, tracers),
                (owner_in, owner),
                (area_in, area),
            )
        )
    ]
    for copy in inputs:
        copy.start()

    def greet(j, carry):
        target = lax.rem(me + j, n)
        pl.semaphore_signal(
            barrier, inc=1, device_id=(target // n_lat, lax.rem(target, n_lat)), device_id_type=MESH
        )
        return carry

    lax.fori_loop(1, n, greet, 0)

    lane = lax.broadcasted_iota(jnp.int32, (nr, nc), 1)
    row = lax.broadcasted_iota(jnp.int32, (nr, nc), 0)

    for copy in inputs:
        copy.wait()

    def pack(k, carry):
        west, east_side = carry
        depth[k] = depth[k] * mask[k].astype(jnp.float32)
        for item in range(nt + 2):
            if item < nt:
                x = tracers[item, k]
            elif item == nt:
                x = depth[k]
            else:
                x = east[k]
            at = item * nl + k
            west = jnp.where(lane == at, x[:, 0:1], west)
            east_side = jnp.where(lane == at, x[:, nc - 1 : nc], east_side)
            y = north[k] if item == nt + 1 else x
            row_pack[0, pl.ds(at, 1), :] = y[0:1, :]
            row_pack[1, pl.ds(at, 1), :] = y[nr - 1 : nr, :]
        return west, east_side

    zero = jnp.zeros((nr, nc), jnp.float32)
    west, east_side = lax.fori_loop(0, nl, pack, (zero, zero))
    col_pack[0] = west
    col_pack[1] = east_side

    at_fold = lat == n_lat - 1
    items = row_pack.shape[1]

    @pl.when(at_fold)
    def _():
        flip = (
            lax.broadcasted_iota(jnp.int32, (nc, nc), 0)
            + lax.broadcasted_iota(jnp.int32, (nc, nc), 1)
            == nc - 1
        )
        turned = exact_dot(row_pack[1], flip.astype(jnp.float32).astype(jnp.bfloat16))
        index = lax.broadcasted_iota(jnp.int32, (items, nc), 0)
        row_pack[1] = jnp.where(index >= (nt + 1) * nl, -turned, turned)

    @pl.when(lat == 0)
    def _():
        row_got[0] = jnp.zeros((items, nc), jnp.float32)

    pl.semaphore_wait(barrier, n - 1)

    def halo(src, dst, at_send, at_recv, to_lon, to_lat):
        return pltpu.make_async_remote_copy(
            src_ref=src,
            dst_ref=dst,
            send_sem=halo_send.at[at_send],
            recv_sem=halo_recv.at[at_recv],
            device_id=(to_lon, to_lat),
            device_id_type=MESH,
        )

    lon_west = lax.rem(lon + n_lon - 1, n_lon)
    lon_east = lax.rem(lon + 1, n_lon)
    to_west = halo(col_pack.at[0], col_got.at[1], 0, 1, lon_west, lat)
    to_east = halo(col_pack.at[1], col_got.at[0], 1, 0, lon_east, lat)
    to_south = halo(row_pack.at[0], row_got.at[1], 2, 3, lon, lat - 1)
    to_north = halo(row_pack.at[1], row_got.at[0], 3, 2, lon, lat + 1)
    to_fold = halo(row_pack.at[1], row_got.at[1], 3, 3, n_lon - 1 - lon, lat)
    to_west.start()
    to_east.start()

    @pl.when(lat > 0)
    def _():
        to_south.start()

    @pl.when(at_fold)
    def _():
        to_fold.start()

    @pl.when(jnp.logical_not(at_fold))
    def _():
        to_north.start()

    def matrix(shape, shift):
        hit = (lax.broadcasted_iota(jnp.int32, shape, 0) >> shift) == lax.broadcasted_iota(
            jnp.int32, shape, 1
        )
        return hit.astype(jnp.float32).astype(jnp.bfloat16)

    pool_two[...] = matrix(pool_two.shape, 1)
    pool_four[...] = matrix(pool_four.shape, 2)

    units = blocks.shape[0]
    unit_a = lax.broadcasted_iota(jnp.int32, (units, units), 0)
    unit_b = lax.broadcasted_iota(jnp.int32, (units, units), 1)
    own_row = owner[...]
    own_wide = jnp.broadcast_to(own_row, (units, units))
    own_col = jnp.sum(jnp.where(unit_a == unit_b, own_wide, 0), axis=1, keepdims=True)
    earlier = jnp.logical_and(own_col == own_wide, unit_a < unit_b)
    rank = jnp.sum(jnp.where(earlier, 1, 0), axis=0, keepdims=True)
    slot = own_row * rows_each + rank
    hit = (
        (lax.broadcasted_iota(jnp.int32, (n * rows_each, units), 0) == slot)
        .astype(jnp.float32)
        .astype(jnp.bfloat16)
    )
    place[...] = jnp.concatenate([hit, hit, hit], axis=1)

    to_west.wait()
    to_east.wait()

    @pl.when(lat > 0)
    def _():
        to_south.wait_send()
        to_north.wait_recv()

    @pl.when(at_fold)
    def _():
        to_fold.wait()

    @pl.when(jnp.logical_not(at_fold))
    def _():
        to_north.wait_send()
        to_south.wait_recv()

    bands = nr // BAND_ROWS
    quads = BAND_ROWS // 4

    def level_out(k):
        return pltpu.make_async_copy(updated.at[:, k], updated_out.at[:, k], out_sem.at[k])

    span = quads * bands

    def around(x, item, k):
        at = item * nl + k
        x_east = jnp.where(
            lane == nc - 1, pltpu.roll(col_got[1], nc - 1 - at, 1), pltpu.roll(x, nc - 1, 1)
        )
        x_west = jnp.where(lane == 0, pltpu.roll(col_got[0], nc - at, 1), pltpu.roll(x, 1, 1))
        return x_east, x_west

    def along(x, item, k):
        at = item * nl + k
        x_north = jnp.where(row == nr - 1, row_got[1, pl.ds(at, 1), :], pltpu.roll(x, nr - 1, 0))
        x_south = jnp.where(row == 0, row_got[0, pl.ds(at, 1), :], pltpu.roll(x, 1, 0))
        return x_north, x_south

    def faces(k):
        kappa = mixing[k]
        h = depth[k]
        u = east[k]
        v = north[k]
        grid_area = area[...]
        gain = time_step / (grid_area * jnp.maximum(h, depth_floor))
        h_east, h_west = around(h, nt, k)
        h_north, h_south = along(h, nt, k)
        u_east, u_west = around(u, nt + 1, k)
        v_north, v_south = along(v, nt + 1, k)

        def face(h_other, a, b):
            speed = 0.5 * (a + b)
            scaled = gain * jnp.minimum(h, h_other)
            return (
                scaled * (jnp.maximum(speed, 0.0) + kappa),
                scaled * (kappa - jnp.minimum(speed, 0.0)),
            )

        out_e, in_e = face(h_east, u, u_east)
        in_w, out_w = face(h_west, u_west, u)
        out_n, in_n = face(h_north, v, v_north)
        in_s, out_s = face(h_south, v_south, v)
        coef[0, k] = in_w
        coef[1, k] = in_e
        coef[2, k] = in_s
        coef[3, k] = in_n
        coef[4, k] = (out_e + out_w) + (out_n + out_s)
        coef[5, k] = grid_area * h

    def step(k, t):
        x = tracers[t, k]
        x_east, x_west = around(x, t, k)
        x_north, x_south = along(x, t, k)
        change = (coef[0, k] * x_west + coef[1, k] * x_east) + (
            coef[2, k] * x_south + coef[3, k] * x_north
        )
        new = x + (change - coef[4, k] * x)
        updated[t, k] = new
        product[t] = new * coef[5, k]

    def pooled(fields):
        upper, lower, whole = [], [], []
        for t in fields:
            both = []
            for i in range(quads):
                four = [
                    product[t, pl.ds(4 * i + j, bands, stride=BAND_ROWS), :] for j in range(4)
                ]
                upper.append(four[0] + four[1])
                lower.append(four[2] + four[3])
                both.append(upper[-1] + lower[-1])
            whole.append(jnp.concatenate(both, axis=1))
        halves = [jnp.concatenate(upper, axis=0), jnp.concatenate(lower, axis=0)]
        two = exact_dot(jnp.concatenate(halves, axis=1), pool_two[...])
        four = exact_dot(jnp.concatenate(whole, axis=0), pool_four[...])
        return two, four

    def rows_at(k, count):
        return pl.ds(pl.multiple_of(k * count, count), count)

    def keep(k, t, two, four):
        at_rows = rows_at(k, bands)
        ratio = two / den_two[rows_at(k, span), :]
        for i in range(quads):
            column = (t * quads + i) * nc
            blocks[at_rows, column : column + nc] = ratio[i * bands : (i + 1) * bands]
        column = (nt * quads + t) * nc
        blocks[at_rows, column : column + nc] = four / den_four[at_rows, :]

    def first(k, carry):
        faces(k)
        product[nt] = coef[5, k]
        step(k, 0)
        two, four = pooled((0, nt))
        den_two[rows_at(k, span), :] = jnp.maximum(two[span:], weight_floor)
        den_four[rows_at(k, bands), :] = jnp.maximum(four[bands:], weight_floor)
        keep(k, 0, two[:span], four[:bands])
        return carry

    def rest(k, carry):
        for t in range(1, nt):
            step(k, t)
        level_out(k).start()
        two, four = pooled(range(1, nt))
        for t in range(1, nt):
            keep(k, t, two[(t - 1) * span : t * span], four[(t - 1) * bands : t * bands])
        return carry

    def placed(send, start, width):
        for at in range(0, width, quads * nc):
            source = blocks[:, start + at : start + at + quads * nc]
            send[:, at : at + quads * nc] = dot(
                place[...], jnp.concatenate(pieces(source), axis=0)
            )

    part = quads * nc
    moves = (
        (send_first, two_out, 0, part),
        (send_rest, two_out, part, (nt - 1) * part),
        (send_four, four_out, 0, nt * nc),
    )
    mine = rows_at(me, rows_each)

    def transfer(index, j, peer, source_rows, target_rows):
        send, out, start, width = moves[index]
        return pltpu.make_async_remote_copy(
            src_ref=send.at[source_rows, :],
            dst_ref=out.at[target_rows, pl.ds(start, width)],
            send_sem=send_sem.at[index, j],
            recv_sem=recv_sem.at[index, j],
            device_id=(peer // n_lat, lax.rem(peer, n_lat)),
            device_id_type=MESH,
        )

    def to_peer(index, j):
        peer = lax.rem(me + j, n)
        return transfer(index, j, peer, rows_at(peer, rows_each), mine)

    def from_peer(index, j):
        peer = lax.rem(me + n - j, n)
        return transfer(index, j, peer, mine, rows_at(peer, rows_each))

    def own_copy(index):
        send, out, start, width = moves[index]
        return pltpu.make_async_copy(
            send.at[mine, :], out.at[mine, pl.ds(start, width)], send_sem.at[index, 0]
        )

    def begin(indices):
        def body(j, carry):
            for index in indices:
                to_peer(index, j).start()
            return carry

        lax.fori_loop(1, n, body, 0)
        for index in indices:
            own_copy(index).start()

    lax.fori_loop(0, nl, first, 0)
    placed(send_first, 0, part)
    begin((0,))
    lax.fori_loop(0, nl, rest, 0)
    placed(send_rest, part, (nt - 1) * part)
    placed(send_four, nt * part, nt * nc)
    begin((1, 2))

    def end_level(k, carry):
        level_out(k).wait()
        return carry

    lax.fori_loop(0, nl, end_level, 0)
    for index in range(3):
        own_copy(index).wait()

    def end(j, carry):
        for index in range(3):
            to_peer(index, j).wait_send()
            from_peer(index, j).wait_recv()
        return carry

    lax.fori_loop(1, n, end, 0)


def local(
    tracers, fill_fraction, ocean_mask, east_speed, north_speed, diffusivity, cell_area, owner_map
):
    nt, nl, nr, nc = tracers.shape
    n_lon = lax.axis_size("lon")
    n_lat = lax.axis_size("lat")
    n = n_lon * n_lat
    units = owner_map.shape[0]
    capacity = max(2, 2 * units // n)
    rows_each = -(-capacity // 8) * 8
    wide_two = nt * BAND_ROWS * nc // 4
    wide_four = nt * BAND_ROWS * nc // 16
    wide = wide_two + wide_four
    items = (nt + 2) * nl
    f32 = jnp.float32
    hbm = pl.BlockSpec(memory_space=pltpu.HBM)
    part = wide_two // nt
    updated, two, four = pl.pallas_call(
        functools.partial(kernel, (n_lon, n_lat, rows_each)),
        out_shape=(
            jax.ShapeDtypeStruct(tracers.shape, f32),
            jax.ShapeDtypeStruct((n * rows_each, wide_two), f32),
            jax.ShapeDtypeStruct((n * rows_each, wide_four), f32),
        ),
        in_specs=[hbm] * 5 + [pl.BlockSpec(memory_space=pltpu.SMEM)] + [hbm] * 2,
        out_specs=(hbm, hbm, hbm),
        scratch_shapes=[
            pltpu.VMEM(tracers.shape, f32),
            pltpu.VMEM((nl, nr, nc), f32),
            pltpu.VMEM((nl, nr, nc), jnp.int32),
            pltpu.VMEM((nl, nr, nc), f32),
            pltpu.VMEM((nl, nr, nc), f32),
            pltpu.VMEM((nr, nc), f32),
            pltpu.VMEM((1, units), jnp.int32),
            pltpu.VMEM(tracers.shape, f32),
            pltpu.VMEM((6, nl, nr, nc), f32),
            pltpu.VMEM((nt + 1, nr, nc), f32),
            pltpu.VMEM((units * BAND_ROWS // 4, nc), f32),
            pltpu.VMEM((units, nc), f32),
            pltpu.VMEM((units, wide), f32),
            pltpu.VMEM((n * rows_each, part), f32),
            pltpu.VMEM((n * rows_each, wide_two - part), f32),
            pltpu.VMEM((n * rows_each, wide_four), f32),
            pltpu.VMEM((n * rows_each, 3 * units), jnp.bfloat16),
            pltpu.VMEM((2 * nc, nc), jnp.bfloat16),
            pltpu.VMEM((4 * nc, nc), jnp.bfloat16),
            pltpu.VMEM((2, nr, nc), f32),
            pltpu.VMEM((2, nr, nc), f32),
            pltpu.VMEM((2, items, nc), f32),
            pltpu.VMEM((2, items, nc), f32),
            pltpu.SemaphoreType.DMA((4,)),
            pltpu.SemaphoreType.DMA((4,)),
            pltpu.SemaphoreType.DMA((3, n)),
            pltpu.SemaphoreType.DMA((3, n)),
            pltpu.SemaphoreType.DMA((nl,)),
            pltpu.SemaphoreType.DMA((7,)),
        ],
        compiler_params=pltpu.CompilerParams(
            collective_id=0, has_side_effects=True, vmem_limit_bytes=56 * 1024 * 1024
        ),
        name="substep",
    )(
        tracers,
        fill_fraction,
        ocean_mask,
        east_speed,
        north_speed,
        diffusivity,
        cell_area,
        owner_map.reshape(1, units),
    )
    if rows_each != capacity:
        two, four = (
            got.reshape(n, rows_each, -1)[:, :capacity].reshape(n * capacity, -1)
            for got in (two, four)
        )
    return updated, two[None], four[None]


def solution(mesh):
    in_specs = (
        P(None, None, "lat", "lon"),
        P(None, "lat", "lon"),
        P(None, "lat", "lon"),
        P(None, "lat", "lon"),
        P(None, "lat", "lon"),
        P(),
        P("lat", "lon"),
        P(("lon", "lat"), None),
    )
    out_specs = (
        P(None, None, "lat", "lon"),
        P(("lon", "lat"), None, None),
        P(("lon", "lat"), None, None),
    )
    return jax.shard_map(local, mesh=mesh, in_specs=in_specs, out_specs=out_specs, check_vma=False)
```

time: 103 us -> 91 us (0.88)
  local copies, waits for them, and re-layouts: 14.3 us -> 6.97 us
  Pallas kernels: 86.3 us -> 82.1 us
    broadcast_in_dim x2 -> x0, local copies, waits for them, and re-layouts: 5.15 us -> none  [local(): return (updated, received[None, :, :wide_two], received[None, :, wide_two:])]
    pallas_call x1, Pallas kernels: 86.3 us -> 82.1 us  [local(): pl.pallas_call(functools.partial(kernel, (n_lon, n_lat, rows_each)), out_...]
    unnamed x16 -> x7, local copies, waits for them, and re-layouts: 9.17 us -> 6.97 us
where the time goes in v2:
time: 91 us; the launch traced here: 89.7 us
  Pallas kernels  82.1 us (90%)
  local copies, waits for them, and re-layouts  6.97 us (8%)
    pallas_call x1, Pallas kernels, local(): pl.pallas_call(functools.partial(kernel, (n_lon, n_lat, rows_each)), out_...  82.1 us
    unnamed x7, local copies, waits for them, and re-layouts  6.97 us

profile of v2, /device:TPU:0, one launch (start us, length us, event | category | flops | bytes accessed | tf_op | source)
XLA Modules:
  0.0 89.7 jit_solution(2859556343427110611)
XLA Ops:
  0.6 82.1 %substep.1 = (f32[4,16,128,128]{3,2,1,0:T(8,128)}, f32[256,2048]{1,0:T(8,128)}, f32[256,512]{1,0:T(8,128)}) custom-call(f32[4,16,128,128]{3,2,1,0:T(8,128)} %tracers_in.1, f32[16,128,128]{2,1,0:T(8,128)} %fill_in.1, s32[16,128,128]{2,1,0:T(8,128)} %mask_in.1, f32[16,128,128]{2,1,0:T(8,128)} %east_in.1, f32[16,128,128]{2,1,0:T(8,128)} %north_in.1, f32[16]{0:T(128)} %mixing.1, ...), custom_call_target="tpu_custom_call" | custom-call | tf_op jit(solution)/shard_map/substep/pallas_call | solution.py:439
  82.7 0.0 copy-start
  82.7 0.0 copy-start.1
  82.7 4.8 %copy.14 = f32[4,16,128,128]{3,2,1,0:T(8,128)} copy(f32[4,16,128,128]{3,2,1,0:T(8,128)} %get-tuple-element.12) | data formatting | bytes 8388608
  87.6 0.0 copy-done
  87.6 1.3 %copy.15 = f32[1,256,2048]{2,1,0:T(8,128)} copy(f32[1,256,2048]{2,1,0:T(8,128)S(1)} %bitcast.3) | data formatting | bytes 4194304
  88.9 0.0 copy-done.1
  88.9 0.8 copy.16
Async XLA Ops:
  82.7 4.9 %copy-start = (f32[256,2048]{1,0:T(8,128)S(1)}, f32[256,2048]{1,0:T(8,128)}, u32[]{:S(2)}) copy-start(f32[256,2048]{1,0:T(8,128)} %get-tuple-element.7) | copy-start | bytes 6291460
  82.7 6.2 %copy-start.1 = (f32[256,512]{1,0:T(8,128)S(1)}, f32[256,512]{1,0:T(8,128)}, u32[]{:S(2)}) copy-start(f32[256,512]{1,0:T(8,128)} %get-tuple-element.8) | copy-start | bytes 1572868
